TPU v7x, 32 devices: a whole 2x2x4 slice. The times are simulated.
32 devices in a mesh: groups: 2 (over x), dp: 16 (over z, y, core).
Axes of the slice: x: 2, y: 2, z: 4, core: 2. Of those that a mesh axis runs over, the one named last changes fastest.
Arguments:
- embeddings: bfloat16 [16384, 1152], P(('groups', 'dp')), parts along dimension 0, may hold values from -600 to 600
- labels: int32 [16384], P(('groups', 'dp')), parts along dimension 0, may hold values from 0 to 31, as said below
Outputs:
- best_match: float32 [16384], P(('groups', 'dp')), parts along dimension 0
There are 2 independent parts, one for each index of `groups`. A program takes and returns all parts, laid end to end along the dimension named above; each array names one. Nothing has to cross between parts.
Inputs may be any that keep to these rules, and one draw needn't show every extreme that they name: `labels`: each device's 512 rows name each cluster at most 32 times, and on every device some cluster exactly 32 times.
All inputs are finite; a program needn't handle non-finite values.
Results may differ from a plain program's by a relative error of at most 0.00045.
Values may be sent and summed in bfloat16 or wider, within the bound.
A program may use at most 128 MiB of HBM per device.

v0:
```python
import jax
import jax.numpy as jnp
from jax import lax
from jax.sharding import PartitionSpec as P

CAP = 32
CL_DEV = 2


def triangle_maxima(packed, filled, block, nblocks):
    places = jnp.arange(block, dtype=jnp.int32)
    pieces = []
    for first in range(nblocks):
        query = packed[first * block : (first + 1) * block]
        running = jnp.full((block,), -1.0, jnp.float32)
        for second in range(first + 1):
            keys = packed[second * block : (second + 1) * block]

            def compute(current, query=query, keys=keys, first=first, second=second):
                scores = jnp.einsum("qd,kd->qk", query, keys, preferred_element_type=jnp.float32)
                query_pos = first * block + places
                key_pos = second * block + places
                keep = (key_pos[None, :] < query_pos[:, None]) & (key_pos[None, :] < filled)
                return jnp.maximum(current, jnp.max(jnp.where(keep, scores, -1.0), axis=1))

            def unchanged(current):
                return current

            running = lax.cond(first * block < filled, compute, unchanged, running)
        pieces.append(running)
    return jnp.concatenate(pieces, axis=0)


def local(embeddings, labels):
    width = embeddings.shape[1]
    peers = lax.axis_size("dp")
    clusters = CL_DEV * peers
    wide = embeddings.astype(jnp.float32)
    unit = (wide * lax.rsqrt(jnp.sum(wide * wide, axis=1, keepdims=True) + 1e-06)).astype(
        jnp.bfloat16
    )
    names = jnp.arange(clusters, dtype=jnp.int32)
    onehot = (labels[:, None] == names[None, :]).astype(jnp.int32)
    rank = jnp.sum((jnp.cumsum(onehot, axis=0) - onehot) * onehot, axis=1)
    local_counts = jnp.sum(onehot, axis=0)
    row_slot = jnp.sum(onehot * names[None, :], axis=1)
    position = row_slot * CAP + rank
    send_rows = jnp.zeros((clusters * CAP, width), jnp.bfloat16).at[position].set(unit)
    send_rows = send_rows.reshape(peers, CL_DEV * CAP, width)
    send_counts = (
        jnp.zeros((clusters,), jnp.int32).at[names].set(local_counts).reshape(peers, CL_DEV)
    )
    got_rows, got_counts = (
        lax.all_to_all(send_rows, "dp", split_axis=0, concat_axis=0, tiled=True),
        lax.all_to_all(send_counts, "dp", split_axis=0, concat_axis=0, tiled=True),
    )
    region = peers * CAP
    block = min(512, region)
    nblocks = region // block
    slot_steps = jnp.arange(CAP, dtype=jnp.int32)
    results = []
    for which in range(CL_DEV):
        part_rows = got_rows[:, which * CAP : (which + 1) * CAP, :].reshape(region, width)
        have = got_counts[:, which]
        start = jnp.cumsum(have) - have
        valid = slot_steps[None, :] < have[:, None]
        target_rows = jnp.where(valid, start[:, None] + slot_steps[None, :], region).reshape(region)
        packed = (
            jnp.zeros((region + 1, width), jnp.bfloat16).at[target_rows].set(part_rows)[:region]
        )
        filled = jnp.sum(have)
        maxima = triangle_maxima(packed, filled, block, nblocks)
        results.append(maxima[jnp.minimum(target_rows, region - 1)].reshape(peers, CAP))
    answers = jnp.concatenate(results, axis=1)
    returned = lax.all_to_all(answers, "dp", split_axis=0, concat_axis=0, tiled=True)
    return returned.reshape(-1)[position]


def solution(mesh):
    in_specs = (P(("groups", "dp"), None), P(("groups", "dp")))
    out_specs = P(("groups", "dp"))
    return jax.shard_map(local, mesh=mesh, in_specs=in_specs, out_specs=out_specs, check_vma=False)
```

profile of v0, /device:TPU:0, one launch (start us, length us, event | category | flops | bytes accessed | tf_op | source)
XLA Modules:
  0.0 111.6 jit_solution(6196879217115084029)
XLA Ops:
  0.0 0.8 fusion.16
  0.8 1.2 %reduce-window.15 = s32[32,4,128]{2,0,1:T(8,128)S(1)} reduce-window(s32[32,4,128]{2,0,1:T(8,128)S(1)} %fusion.16, s32[]{:T(128)} %constant.21.clone.1), window={size=1x1x128 pad=0_0x0_0x127_0}, to_apply=%region_5.6 | reduce-window | flops 2080768 | bytes 131076 | tf_op jit(solution)/shard_map/reduce-window.1
  2.2 0.9 select_reduce_fusion
  3.1 0.7 scatter_custom_fusion
  3.8 0.7 all_to_all.17
  4.5 7.4 %all-to-all-start = ((s32[16,1,2]{2,1,0:T(1,128)}), s32[16,1,2]{2,1,0:T(1,128)S(1)}, u32[]{:S(2)}, u32[]{:S(2)}) async-start(s32[16,1,2]{2,1,0:T(1,128)} %bitcast), calls=%async_computation | async-start | bytes 16384 | tf_op jit(solution)/shard_map/all_to_all | solution.py:55
  11.9 1.6 %fusion.4 = f32[512]{0:T(512)S(1)} fusion(bf16[512,1152]{1,0:T(8,128)(2,1)} %param.6), kind=kLoop, calls=%fused_computation.19 | loop fusion | flops 1768960 | bytes 1181696 | tf_op jit(solution)/shard_map/reduce_sum | solution.py:39
  13.5 4.4 %scatter_custom_fusion.1 = bf16[1024,1152]{1,0:T(8,128)(2,1)} fusion(s32[512]{0:T(512)S(1)} %bitcast.34, bf16[512,1152]{1,0:T(8,128)(2,1)S(1)} %copy-done, f32[512]{0:T(512)S(1)} %add_rsqrt_fusion, bf16[]{:T(256)} %constant.22.clone.1), kind=kCustom, calls=%fused_computation.21 | custom fusion | flops 1769472 | bytes 3540994 | tf_op jit(solution)/shard_map/scatter | solution.py:48
  18.3 5.6 %all-to-all-start.1 = ((bf16[16,64,1152]{2,1,0:T(8,128)(2,1)}), bf16[16,64,1152]{2,1,0:T(8,128)(2,1)S(1)}, u32[]{:S(2)}, u32[]{:S(2)}) async-start(bf16[16,64,1152]{2,1,0:T(8,128)(2,1)} %bitcast.28), calls=%async_computation.1 | async-start | bytes 4718592 | tf_op jit(solution)/shard_map/all_to_all | solution.py:54
  27.1 42.4 %all-to-all-done.1 = bf16[16,64,1152]{2,1,0:T(8,128)(2,1)S(1)} async-done(((bf16[16,64,1152]{2,1,0:T(8,128)(2,1)}), bf16[16,64,1152]{2,1,0:T(8,128)(2,1)S(1)}, u32[]{:S(2)}, u32[]{:S(2)}) %all-to-all-start.1) | async-done | bytes 2359328 | tf_op jit(solution)/shard_map/all_to_all | solution.py:54
  69.5 1.2 %fusion.19 = (bf16[16,32,1152]{2,1,0:T(8,128)(2,1)}, bf16[16,32,1152]{2,1,0:T(8,128)(2,1)S(1)}) fusion(bf16[16,64,1152]{2,1,0:T(8,128)(2,1)S(1)} %all-to-all-done.1), kind=kLoop, calls=%fused_computation.62 | loop fusion | bytes 4718592 | tf_op jit(solution)/shard_map/slice | solution.py:63
  70.7 3.6 %scatter_custom_fusion.2 = bf16[513,1152]{1,0:T(8,128)(2,1)S(1)} fusion(s32[512]{0:T(512)} %bitcast.39, bf16[512,1152]{1,0:T(8,128)(2,1)} %bitcast.30, bf16[]{:T(256)} %constant.22.clone.1), kind=kCustom, calls=%fused_computation.26 | custom fusion | bytes 1182464 | tf_op jit(solution)/shard_map/scatter | solution.py:69
  74.3 1.6 %conditional.2 = (f32[512]{0:T(512)S(1)}) conditional(s32[]{:T(128)} %convert_element_type.20, () %tuple.17, (s32[512]{0:T(512)S(1)}, s32[]{:T(128)}, s32[512]{0:T(512)S(1)}, bf16[513,1152]{1,0:T(8,128)(2,1)S(1)}) %tuple.18), branch_computations={%region_11.12_spmd, %region_12.14_spmd} | conditional | flops 605028864 | bytes 1192972 | solution.py:29
  75.0 0.9 fusion
  75.9 3.5 %gather_fusion = f32[512]{0:T(512)S(1)} fusion(f32[512]{0:T(512)S(1)} %get-tuple-element.52, s32[1024]{0:T(1024)S(1)} %pad_clamp_fusion.2), kind=kCustom, calls=%fused_computation | custom fusion | bytes 6144 | tf_op jit(solution)/shard_map/gather | solution.py:73
  79.5 2.9 %scatter_custom_fusion.3 = bf16[513,1152]{1,0:T(8,128)(2,1)S(1)} fusion(s32[512]{0:T(512)S(1)} %bitcast.38, bf16[512,1152]{1,0:T(8,128)(2,1)S(1)} %bitcast.29, bf16[]{:T(256)} %constant.22.clone.1), kind=kCustom, calls=%fused_computation.24 | custom fusion | bytes 1181954 | tf_op jit(solution)/shard_map/scatter | solution.py:69
  82.4 1.5 %conditional.3 = (f32[512]{0:T(512)S(1)}) conditional(s32[]{:T(128)} %convert_element_type.24, () %tuple.19, (s32[512]{0:T(512)S(1)}, s32[]{:T(128)}, s32[512]{0:T(512)S(1)}, bf16[513,1152]{1,0:T(8,128)(2,1)S(1)}) %tuple.20), branch_computations={%region_17.18_spmd, %region_18.20_spmd} | conditional | flops 605028864 | bytes 1192972 | solution.py:29
  83.0 0.9 fusion.2
  83.9 3.5 %gather_fusion.1 = f32[512]{0:T(512)S(1)} fusion(f32[512]{0:T(512)S(1)} %get-tuple-element.53, s32[1024]{0:T(1024)S(1)} %pad_clamp_fusion.1), kind=kCustom, calls=%fused_computation.1 | custom fusion | bytes 6144 | tf_op jit(solution)/shard_map/gather | solution.py:73
  87.5 0.7 pad_maximum_fusion
  88.2 12.3 %all-to-all-start.2 = ((f32[16,1,64]{2,1,0:T(1,128)}), f32[16,1,64]{2,1,0:T(1,128)S(1)}, u32[]{:S(2)}, u32[]{:S(2)}) async-start(f32[16,1,64]{2,1,0:T(1,128)} %bitcast.13), calls=%async_computation.2 | async-start | bytes 16384 | tf_op jit(solution)/shard_map/all_to_all | solution.py:75
  100.5 6.4 %all-to-all-done.2 = f32[16,1,64]{2,1,0:T(1,128)S(1)} async-done(((f32[16,1,64]{2,1,0:T(1,128)}), f32[16,1,64]{2,1,0:T(1,128)S(1)}, u32[]{:S(2)}, u32[]{:S(2)}) %all-to-all-start.2) | async-done | bytes 4128 | tf_op jit(solution)/shard_map/all_to_all | solution.py:75
  107.4 0.7 reduce.13
  108.1 3.4 %gather_fusion.2 = f32[512]{0:T(512)} fusion(f32[1024]{0:T(1024)S(1)} %reshape.259, s32[1024]{0:T(1024)S(1)} %pad_clamp_fusion), kind=kCustom, calls=%fused_computation.2 | custom fusion | bytes 6144 | tf_op jit(solution)/shard_map/gather | solution.py:76
  (36 shorter events, 4.7 us)
Async XLA Ops:
  0.0 13.5 %copy-start = (bf16[512,1152]{1,0:T(8,128)(2,1)S(1)}, bf16[512,1152]{1,0:T(8,128)(2,1)}, u32[]{:S(2)}) copy-start(bf16[512,1152]{1,0:T(8,128)(2,1)} %param.6) | copy-start | bytes 3538948
  4.5 13.8 %all-to-all-start = ((s32[16,1,2]{2,1,0:T(1,128)}), s32[16,1,2]{2,1,0:T(1,128)S(1)}, u32[]{:S(2)}, u32[]{:S(2)}) async-start(s32[16,1,2]{2,1,0:T(1,128)} %bitcast), calls=%async_computation | async-start | bytes 16384 | tf_op jit(solution)/shard_map/all_to_all | solution.py:55
  18.3 51.3 %all-to-all-start.1 = ((bf16[16,64,1152]{2,1,0:T(8,128)(2,1)}), bf16[16,64,1152]{2,1,0:T(8,128)(2,1)S(1)}, u32[]{:S(2)}, u32[]{:S(2)}) async-start(bf16[16,64,1152]{2,1,0:T(8,128)(2,1)} %bitcast.28), calls=%async_computation.1 | async-start | bytes 4718592 | tf_op jit(solution)/shard_map/all_to_all | solution.py:54
  88.2 18.7 %all-to-all-start.2 = ((f32[16,1,64]{2,1,0:T(1,128)}), f32[16,1,64]{2,1,0:T(1,128)S(1)}, u32[]{:S(2)}, u32[]{:S(2)}) async-start(f32[16,1,64]{2,1,0:T(1,128)} %bitcast.13), calls=%async_computation.2 | async-start | bytes 16384 | tf_op jit(solution)/shard_map/all_to_all | solution.py:75
where the time goes:
time: 112 us
  waiting for transfers between devices  49.2 us (44%)
  starting transfers between devices  25.2 us (22%)
  local copies, waits for them, and re-layouts  20.8 us (19%)
  other arithmetic  13 us (12%)
  matrix products  1.84 us (2%)
  between operations  1.37 us (1%)
    all_to_all x1, waiting for transfers between devices, local(): lax.all_to_all(send_rows, 'dp', split_axis=0, concat_axis=0, tiled=True)  42.4 us
    all_to_all x1, starting transfers between devices, local(): lax.all_to_all(answers, 'dp', split_axis=0, concat_axis=0, tiled=True)  12.3 us
    all_to_all x1, starting transfers between devices, local(): lax.all_to_all(send_counts, 'dp', split_axis=0, concat_axis=0, tiled=True)  7.39 us
    gather x2, local copies, waits for them, and re-layouts, local(): maxima[jnp.minimum(target_rows, region - 1)].reshape(peers, CAP)  7.03 us
    scatter x2, local copies, waits for them, and re-layouts, local(): jnp.zeros((region + 1, width), jnp.bfloat16).at[target_rows].set(part_rows)  6.44 us
    all_to_all x1, waiting for transfers between devices, local(): lax.all_to_all(answers, 'dp', split_axis=0, concat_axis=0, tiled=True)  6.39 us
    all_to_all x1, starting transfers between devices, local(): lax.all_to_all(send_rows, 'dp', split_axis=0, concat_axis=0, tiled=True)  5.58 us
    scatter x1, other arithmetic, local(): jnp.zeros((clusters * CAP, width), jnp.bfloat16).at[position].set(unit)  4.36 us
  transfers between devices with their start and end apart: 3, of which 3 were waited for; matrix products, arithmetic and copies ran while one was open for 7% of the time, Pallas kernels for 0%

commit v1 on v0

v1 whole, which is shorter than its diff:
```python
import functools

import jax
import jax.numpy as jnp
from jax import lax
from jax.experimental import pallas as pl
from jax.experimental.pallas import tpu as pltpu
from jax.sharding import PartitionSpec as P

CAP = 32
CL_DEV = 2
MESH = pl.DeviceIdType.MESH
SEND = CAP * CL_DEV
EMPTY = 2.0


def flip(me, k, n):
    total = 0
    bit = 1
    while bit < n:
        have = (me // bit) % 2
        total = total + ((1 - have) if (k // bit) % 2 else have) * bit
        bit *= 2
    return total


def kernel(n, rows, emb_ref, lab_ref, out_ref, unit, packed, got, mine, back, send_sem, recv_sem, bsend_sem, brecv_sem, own_sem):
    me = lax.axis_index("dp")
    group = lax.axis_index("groups")
    region = n * CAP
    strips = region // 128

    barrier = pltpu.get_barrier_semaphore()
    for k in range(1, n):
        pl.semaphore_signal(barrier, inc=1, device_id=(group, flip(me, k, n)), device_id_type=MESH)

    wide = emb_ref[...].astype(jnp.float32)
    unit[...] = (wide * lax.rsqrt(jnp.sum(wide * wide, axis=1, keepdims=True) + 1e-06)).astype(jnp.bfloat16)

    label = lab_ref[...]
    onehot = lax.broadcasted_iota(jnp.int32, (n * CL_DEV, rows), 0) == label
    before = lax.broadcasted_iota(jnp.int32, (rows, rows), 0) < lax.broadcasted_iota(jnp.int32, (rows, rows), 1)
    ranks = jnp.dot(
        onehot.astype(jnp.bfloat16), before.astype(jnp.bfloat16), preferred_element_type=jnp.float32
    )
    rank = jnp.sum(jnp.where(onehot, ranks, 0.0), axis=0, keepdims=True).astype(jnp.int32)
    position = label * CAP + rank

    per = min(4, n)
    width = emb_ref.shape[1]
    slot = lax.broadcasted_iota(jnp.int32, (SEND, rows), 0)
    first_lane = lax.broadcasted_iota(jnp.int32, (per * SEND, 128), 1) == 0
    copies = {}
    for chunk in reversed(range(n // per)):
        picks = []
        for k in range(chunk * per, (chunk + 1) * per):
            picks.append((position - flip(me, k, n) * SEND) == slot)
        pick = jnp.concatenate([p.astype(jnp.float32) for p in picks], axis=0)
        used = jnp.sum(pick, axis=1, keepdims=True)
        block = jnp.dot(pick.astype(jnp.bfloat16), unit[...], preferred_element_type=jnp.float32)
        head = jnp.where(first_lane, block[:, :128] + EMPTY * (1.0 - used), block[:, :128])
        at = pl.ds(chunk * per * SEND, per * SEND)
        packed[at, :128] = head.astype(jnp.bfloat16)
        packed[at, 128:] = block[:, 128:].astype(jnp.bfloat16)
        if chunk == n // per - 1:
            pl.semaphore_wait(barrier, n - 1)
        for k in reversed(range(chunk * per, (chunk + 1) * per)):
            src = packed.at[pl.ds(k * SEND, SEND)]
            if k == 0:
                copy = pltpu.make_async_copy(src, got.at[me], own_sem)
            else:
                copy = pltpu.make_async_remote_copy(
                    src_ref=src,
                    dst_ref=got.at[me],
                    send_sem=send_sem.at[k],
                    recv_sem=recv_sem.at[k],
                    device_id=(group, flip(me, k, n)),
                    device_id_type=MESH,
                )
            copy.start()
            copies[k] = copy
    copies[0].wait()
    for k in range(1, n):
        copies[k].wait_recv()

    block = min(256, region)
    per_block = block // CAP
    key_place = lax.broadcasted_iota(jnp.int32, (block, block), 0)
    query_place = lax.broadcasted_iota(jnp.int32, (block, block), 1)
    for c in range(CL_DEV):
        part = pl.ds(c * CAP, CAP)
        for qb in range(region // block):
            query = got[pl.ds(qb * per_block, per_block), part, :].reshape(block, width)
            best = jnp.full((1, block), -1.0, jnp.float32)
            for kb in range(qb + 1):
                keys = got[pl.ds(kb * per_block, per_block), part, :].reshape(block, width)
                scores = lax.dot_general(
                    keys, query, (((1,), (1,)), ((), ())), preferred_element_type=jnp.float32
                )
                keep = keys[:, :1].astype(jnp.float32) < 1.5
                if kb == qb:
                    keep = keep & (key_place < query_place)
                best = jnp.maximum(best, jnp.max(jnp.where(keep, scores, -1.0), axis=0, keepdims=True))
            for part_of in range(block // 128):
                mine[pl.ds(c * strips + qb * (block // 128) + part_of, 1), :] = best[
                    :, part_of * 128 : (part_of + 1) * 128
                ]

    returns = []
    for k in reversed(range(1, n)):
        copy = pltpu.make_async_remote_copy(
            src_ref=mine,
            dst_ref=back.at[me],
            send_sem=bsend_sem.at[k],
            recv_sem=brecv_sem.at[k],
            device_id=(group, flip(me, k, n)),
            device_id_type=MESH,
        )
        copy.start()
        returns.append(copy)
    own = pltpu.make_async_copy(mine, back.at[me], own_sem)
    own.start()
    own.wait()
    for k in range(1, n):
        copies[k].wait_send()
    for copy in returns:
        copy.wait()

    strip = (me * CAP) // 128
    lane = (me * CAP) % 128
    home = lax.broadcasted_iota(jnp.int32, (n, rows), 0) * CL_DEV
    spread = jnp.zeros((128, rows), jnp.float32)
    for c in range(CL_DEV):
        table = back[:, pl.ds(c * strips + strip, 1), :].reshape(n, 128)
        spread = spread + lax.dot_general(
            table,
            ((home + c) == label).astype(jnp.float32),
            (((0,), (0,)), ((), ())),
            preferred_element_type=jnp.float32,
            precision=lax.Precision.HIGHEST,
        )
    place = lax.broadcasted_iota(jnp.int32, (128, rows), 0) == (rank + lane)
    out_ref[...] = jnp.sum(jnp.where(place, spread, 0.0), axis=0, keepdims=True)


def solution(mesh):
    n = mesh.shape["dp"]

    def local(embeddings, labels):
        rows, width = embeddings.shape
        tile = (CL_DEV * n * CAP // 128, 128)
        best = pl.pallas_call(
            functools.partial(kernel, n, rows),
            out_shape=jax.ShapeDtypeStruct((1, rows), jnp.float32),
            in_specs=[pl.BlockSpec(memory_space=pltpu.VMEM)] * 2,
            out_specs=pl.BlockSpec(memory_space=pltpu.VMEM),
            scratch_shapes=[
                pltpu.VMEM((rows, width), jnp.bfloat16),
                pltpu.VMEM((n * SEND, width), jnp.bfloat16),
                pltpu.VMEM((n, SEND, width), jnp.bfloat16),
                pltpu.VMEM(tile, jnp.float32),
                pltpu.VMEM((n,) + tile, jnp.float32),
                pltpu.SemaphoreType.DMA((n,)),
                pltpu.SemaphoreType.DMA((n,)),
                pltpu.SemaphoreType.DMA((n,)),
                pltpu.SemaphoreType.DMA((n,)),
                pltpu.SemaphoreType.DMA,
            ],
            compiler_params=pltpu.CompilerParams(
                collective_id=0, has_side_effects=True, vmem_limit_bytes=56 * 1024 * 1024
            ),
        )(embeddings, labels.reshape(1, rows))
        return best.reshape(rows)

    in_specs = (P(("groups", "dp"), None), P(("groups", "dp")))
    return jax.shard_map(local, mesh=mesh, in_specs=in_specs, out_specs=P(("groups", "dp")), check_vma=False)
```

time: 112 us -> 72.2 us (0.64)
  Pallas kernels: 0 us -> 70.8 us
  waiting for transfers between devices: 49.2 us -> 0 us
  starting transfers between devices: 25.2 us -> 0 us
  local copies, waits for them, and re-layouts: 20.8 us -> 1.26 us
  other arithmetic: 13 us -> 0 us
  matrix products: 1.84 us -> 0 us
  between operations: 1.37 us -> 0.01 us
    pallas_call x0 -> x1, Pallas kernels: none -> 70.8 us  [local(): pl.pallas_call(functools.partial(kernel, n, rows), out_shape=jax.ShapeDty...]
    all_to_all x3 -> x0, waiting for transfers between devices: 49.2 us -> none  [the longest x1 42.4 us: local(): lax.all_to_all(send_rows, 'dp', split_axis=0, concat_axis=0, tiled=True)]
    all_to_all x3 -> x0, starting transfers between devices: 25.2 us -> none  [the longest x1 12.3 us: local(): lax.all_to_all(answers, 'dp', split_axis=0, concat_axis=0, tiled=True)]
    gather x3 -> x0, local copies, waits for them, and re-layouts: 10.4 us -> none  [the longest x2 7.03 us: local(): maxima[jnp.minimum(target_rows, region - 1)].reshape(peers, CAP)]
    scatter x3 -> x0, local copies, waits for them, and re-layouts: 7.12 us -> none  [the longest x2 6.44 us: local(): jnp.zeros((region + 1, width), jnp.bfloat16).at[target_rows].set(part_rows)]
    scatter x1 -> x0, other arithmetic: 4.36 us -> none  [local(): jnp.zeros((clusters * CAP, width), jnp.bfloat16).at[position].set(unit)]
    reduce_sum x3 -> x0, other arithmetic: 3.12 us -> none  [the longest x1 1.58 us: local(): jnp.sum(wide * wide, axis=1, keepdims=True) + 1e-06]
    dot_general x2 -> x0, matrix products: 1.84 us -> none  [compute(): jnp.einsum('qd,kd->qk', query, keys, preferred_element_type=jnp.float32)]
  transfers between devices with their start and end apart: 3 -> 0, of which waited for: 3 -> 0; matrix products, arithmetic and copies ran while one was open for 7% -> 0% of each run, Pallas kernels for 0% -> 0%
where the time goes in v1:
time: 72.2 us; the launch traced here: 72 us
  Pallas kernels  70.8 us (98%)
  local copies, waits for them, and re-layouts  1.26 us (2%)
    pallas_call x1, Pallas kernels, local(): pl.pallas_call(functools.partial(kernel, n, rows), out_shape=jax.ShapeDty...  70.8 us

profile of v1, /device:TPU:0, one launch (start us, length us, event | category | flops | bytes accessed | tf_op | source)
XLA Modules:
  0.0 72.0 jit_solution(412753644889025618)
XLA Ops:
  0.0 70.8 %shard_map.28 = f32[1,512]{1,0:T(1,128)} custom-call(bf16[512,1152]{1,0:T(8,128)(2,1)} %emb_ref.1, s32[1,512]{1,0:T(1,128)} %bitcast.3), custom_call_target="tpu_custom_call" | custom-call | tf_op jit(solution)/shard_map/pallas_call | solution.py:152
  70.8 1.3 %copy.4 = f32[512]{0:T(512)} copy(f32[512]{0:T(512)} %bitcast.2) | data formatting | bytes 4096

commit v2 on v1

--- a/solution.py
+++ b/solution.py
@@ -12,6 +12,7 @@
 MESH = pl.DeviceIdType.MESH
 SEND = CAP * CL_DEV
 EMPTY = 2.0
+PER = 4
 
 
 def flip(me, k, n):
@@ -46,30 +47,30 @@
     rank = jnp.sum(jnp.where(onehot, ranks, 0.0), axis=0, keepdims=True).astype(jnp.int32)
     position = label * CAP + rank
 
-    per = min(4, n)
     width = emb_ref.shape[1]
+    groups = n // PER
+    half = groups // 2
     slot = lax.broadcasted_iota(jnp.int32, (SEND, rows), 0)
-    first_lane = lax.broadcasted_iota(jnp.int32, (per * SEND, 128), 1) == 0
+    first_lane = lax.broadcasted_iota(jnp.int32, (PER * SEND, 128), 1) == 0
     copies = {}
-    for chunk in reversed(range(n // per)):
-        picks = []
-        for k in range(chunk * per, (chunk + 1) * per):
-            picks.append((position - flip(me, k, n) * SEND) == slot)
+    for chunk in [half] + list(range(half)) + list(range(half + 1, groups)):
+        mates = range(chunk * PER, (chunk + 1) * PER)
+        picks = [(position - flip(me, k, n) * SEND) == slot for k in mates]
         pick = jnp.concatenate([p.astype(jnp.float32) for p in picks], axis=0)
         used = jnp.sum(pick, axis=1, keepdims=True)
         block = jnp.dot(pick.astype(jnp.bfloat16), unit[...], preferred_element_type=jnp.float32)
         head = jnp.where(first_lane, block[:, :128] + EMPTY * (1.0 - used), block[:, :128])
-        at = pl.ds(chunk * per * SEND, per * SEND)
+        at = pl.ds(chunk * PER * SEND, PER * SEND)
         packed[at, :128] = head.astype(jnp.bfloat16)
         packed[at, 128:] = block[:, 128:].astype(jnp.bfloat16)
-        if chunk == n // per - 1:
+        if chunk == half:
             pl.semaphore_wait(barrier, n - 1)
-        for k in reversed(range(chunk * per, (chunk + 1) * per)):
+        for k in mates:
             src = packed.at[pl.ds(k * SEND, SEND)]
             if k == 0:
-                copy = pltpu.make_async_copy(src, got.at[me], own_sem)
+                copies[k] = pltpu.make_async_copy(src, got.at[me], own_sem)
             else:
-                copy = pltpu.make_async_remote_copy(
+                copies[k] = pltpu.make_async_remote_copy(
                     src_ref=src,
                     dst_ref=got.at[me],
                     send_sem=send_sem.at[k],
@@ -77,34 +78,41 @@
                     device_id=(group, flip(me, k, n)),
                     device_id_type=MESH,
                 )
-            copy.start()
-            copies[k] = copy
-    copies[0].wait()
-    for k in range(1, n):
-        copies[k].wait_recv()
+            copies[k].start()
 
-    block = min(256, region)
-    per_block = block // CAP
-    key_place = lax.broadcasted_iota(jnp.int32, (block, block), 0)
-    query_place = lax.broadcasted_iota(jnp.int32, (block, block), 1)
-    for c in range(CL_DEV):
-        part = pl.ds(c * CAP, CAP)
-        for qb in range(region // block):
-            query = got[pl.ds(qb * per_block, per_block), part, :].reshape(block, width)
-            best = jnp.full((1, block), -1.0, jnp.float32)
-            for kb in range(qb + 1):
-                keys = got[pl.ds(kb * per_block, per_block), part, :].reshape(block, width)
+    mine[...] = jnp.full(mine.shape, -1.0, jnp.float32)
+    span = PER * CAP
+    earlier = lax.broadcasted_iota(jnp.int32, (span, span), 0) < lax.broadcasted_iota(jnp.int32, (span, span), 1)
+    my_group = me // PER
+    for chunk in range(groups):
+        for k in range(chunk * PER, (chunk + 1) * PER):
+            if k == 0:
+                copies[k].wait()
+            else:
+                copies[k].wait_recv()
+        new = flip(my_group, chunk, groups)
+        for other in range(chunk + 1):
+            old = flip(my_group, other, groups)
+            if other == chunk:
+                low, high = new, new
+            else:
+                top = 1 << ((chunk ^ other).bit_length() - 1)
+                later = (new // top) % 2
+                low = new * (1 - later) + old * later
+                high = new * later + old * (1 - later)
+            for c in range(CL_DEV):
+                part = pl.ds(c * CAP, CAP)
+                keys = got[pl.ds(low * PER, PER), part, :].reshape(span, width)
+                query = got[pl.ds(high * PER, PER), part, :].reshape(span, width)
                 scores = lax.dot_general(
                     keys, query, (((1,), (1,)), ((), ())), preferred_element_type=jnp.float32
                 )
                 keep = keys[:, :1].astype(jnp.float32) < 1.5
-                if kb == qb:
-                    keep = keep & (key_place < query_place)
-                best = jnp.maximum(best, jnp.max(jnp.where(keep, scores, -1.0), axis=0, keepdims=True))
-            for part_of in range(block // 128):
-                mine[pl.ds(c * strips + qb * (block // 128) + part_of, 1), :] = best[
-                    :, part_of * 128 : (part_of + 1) * 128
-                ]
+                if other == chunk:
+                    keep = keep & earlier
+                best = jnp.max(jnp.where(keep, scores, -1.0), axis=0, keepdims=True)
+                line = pl.ds(c * strips + high, 1)
+                mine[line, :] = jnp.maximum(mine[line, :], best)
 
     returns = []
     for k in reversed(range(1, n)):
@@ -170,7 +178,7 @@
                 collective_id=0, has_side_effects=True, vmem_limit_bytes=56 * 1024 * 1024
             ),
         )(embeddings, labels.reshape(1, rows))
-        return best.reshape(rows)
+        return jnp.maximum(best.reshape(rows), -1.0)
 
     in_specs = (P(("groups", "dp"), None), P(("groups", "dp")))
     return jax.shard_map(local, mesh=mesh, in_specs=in_specs, out_specs=P(("groups", "dp")), check_vma=False)

time: 72.2 us -> 68 us (0.942)
  Pallas kernels: 70.8 us -> 66.5 us
  other arithmetic: 0 us -> 1.26 us
  local copies, waits for them, and re-layouts: 1.26 us -> 0 us
    pallas_call x1, Pallas kernels: 70.8 us -> 66.5 us  [local(): pl.pallas_call(functools.partial(kernel, n, rows), out_shape=jax.ShapeDty...]
    max x0 -> x1, other arithmetic: none -> 1.26 us  [local(): return jnp.maximum(best.reshape(rows), -1.0)]
    unnamed x1 -> x0, local copies, waits for them, and re-layouts: 1.26 us -> none
where the time goes in v2:
time: 68 us; the launch traced here: 67.8 us
  Pallas kernels  66.5 us (98%)
  other arithmetic  1.26 us (2%)
    pallas_call x1, Pallas kernels, local(): pl.pallas_call(functools.partial(kernel, n, rows), out_shape=jax.ShapeDty...  66.5 us

profile of v2, /device:TPU:0, one launch (start us, length us, event | category | flops | bytes accessed | tf_op | source)
XLA Modules:
  0.0 67.8 jit_solution(5550753570219494744)
XLA Ops:
  0.0 66.5 %shard_map.28 = f32[1,512]{1,0:T(1,128)} custom-call(bf16[512,1152]{1,0:T(8,128)(2,1)} %emb_ref.1, s32[1,512]{1,0:T(1,128)} %bitcast.2), custom_call_target="tpu_custom_call" | custom-call | tf_op jit(solution)/shard_map/pallas_call | solution.py:160
  66.5 1.3 %broadcast_maximum_fusion = f32[1,512]{1,0:T(1,128)} fusion(f32[1,512]{1,0:T(1,128)} %shard_map.28), kind=kLoop, calls=%fused_computation | loop fusion | flops 512 | bytes 4096 | tf_op jit(solution)/shard_map/max | solution.py:181

commit v3 on v2

--- a/solution.py
+++ b/solution.py
@@ -11,7 +11,7 @@
 CL_DEV = 2
 MESH = pl.DeviceIdType.MESH
 SEND = CAP * CL_DEV
-EMPTY = 2.0
+EMPTY = 32768.0
 PER = 4
 
 
@@ -25,18 +25,13 @@
     return total
 
 
-def kernel(n, rows, emb_ref, lab_ref, out_ref, unit, packed, got, mine, back, send_sem, recv_sem, bsend_sem, brecv_sem, own_sem):
+def kernel(n, rows, emb_ref, lab_ref, out_ref, packed, got, mine, back, send_sem, recv_sem, bsend_sem, brecv_sem, own_sem):
     me = lax.axis_index("dp")
     group = lax.axis_index("groups")
-    region = n * CAP
-    strips = region // 128
 
     barrier = pltpu.get_barrier_semaphore()
     for k in range(1, n):
         pl.semaphore_signal(barrier, inc=1, device_id=(group, flip(me, k, n)), device_id_type=MESH)
-
-    wide = emb_ref[...].astype(jnp.float32)
-    unit[...] = (wide * lax.rsqrt(jnp.sum(wide * wide, axis=1, keepdims=True) + 1e-06)).astype(jnp.bfloat16)
 
     label = lab_ref[...]
     onehot = lax.broadcasted_iota(jnp.int32, (n * CL_DEV, rows), 0) == label
@@ -58,7 +53,7 @@
         picks = [(position - flip(me, k, n) * SEND) == slot for k in mates]
         pick = jnp.concatenate([p.astype(jnp.float32) for p in picks], axis=0)
         used = jnp.sum(pick, axis=1, keepdims=True)
-        block = jnp.dot(pick.astype(jnp.bfloat16), unit[...], preferred_element_type=jnp.float32)
+        block = jnp.dot(pick.astype(jnp.bfloat16), emb_ref[...], preferred_element_type=jnp.float32)
         head = jnp.where(first_lane, block[:, :128] + EMPTY * (1.0 - used), block[:, :128])
         at = pl.ds(chunk * PER * SEND, PER * SEND)
         packed[at, :128] = head.astype(jnp.bfloat16)
@@ -90,6 +85,11 @@
                 copies[k].wait()
             else:
                 copies[k].wait_recv()
+            arrived = pl.ds(flip(me, k, n), 1)
+            wide = got[arrived].reshape(SEND, width).astype(jnp.float32)
+            scale = lax.rsqrt(jnp.sum(wide * wide, axis=1, keepdims=True) + 1e-06)
+            scale = jnp.where(wide[:, :1] < EMPTY / 2, scale, 1.0)
+            got[arrived] = (wide * scale).astype(jnp.bfloat16).reshape(1, SEND, width)
         new = flip(my_group, chunk, groups)
         for other in range(chunk + 1):
             old = flip(my_group, other, groups)
@@ -107,26 +107,27 @@
                 scores = lax.dot_general(
                     keys, query, (((1,), (1,)), ((), ())), preferred_element_type=jnp.float32
                 )
-                keep = keys[:, :1].astype(jnp.float32) < 1.5
+                keep = keys[:, :1].astype(jnp.float32) < EMPTY / 2
                 if other == chunk:
                     keep = keep & earlier
                 best = jnp.max(jnp.where(keep, scores, -1.0), axis=0, keepdims=True)
-                line = pl.ds(c * strips + high, 1)
-                mine[line, :] = jnp.maximum(mine[line, :], best)
+                line = pl.ds(high, 1)
+                mine[line, c, :] = jnp.maximum(mine[line, c, :], best)
 
     returns = []
     for k in reversed(range(1, n)):
+        peer = flip(me, k, n)
         copy = pltpu.make_async_remote_copy(
-            src_ref=mine,
+            src_ref=mine.at[peer // PER],
             dst_ref=back.at[me],
             send_sem=bsend_sem.at[k],
             recv_sem=brecv_sem.at[k],
-            device_id=(group, flip(me, k, n)),
+            device_id=(group, peer),
             device_id_type=MESH,
         )
         copy.start()
         returns.append(copy)
-    own = pltpu.make_async_copy(mine, back.at[me], own_sem)
+    own = pltpu.make_async_copy(mine.at[my_group], back.at[me], own_sem)
     own.start()
     own.wait()
     for k in range(1, n):
@@ -134,12 +135,11 @@
     for copy in returns:
         copy.wait()
 
-    strip = (me * CAP) // 128
-    lane = (me * CAP) % 128
+    lane = (me % PER) * CAP
     home = lax.broadcasted_iota(jnp.int32, (n, rows), 0) * CL_DEV
     spread = jnp.zeros((128, rows), jnp.float32)
     for c in range(CL_DEV):
-        table = back[:, pl.ds(c * strips + strip, 1), :].reshape(n, 128)
+        table = back[:, c, :]
         spread = spread + lax.dot_general(
             table,
             ((home + c) == label).astype(jnp.float32),
@@ -156,18 +156,16 @@
 
     def local(embeddings, labels):
         rows, width = embeddings.shape
-        tile = (CL_DEV * n * CAP // 128, 128)
         best = pl.pallas_call(
             functools.partial(kernel, n, rows),
             out_shape=jax.ShapeDtypeStruct((1, rows), jnp.float32),
             in_specs=[pl.BlockSpec(memory_space=pltpu.VMEM)] * 2,
             out_specs=pl.BlockSpec(memory_space=pltpu.VMEM),
             scratch_shapes=[
-                pltpu.VMEM((rows, width), jnp.bfloat16),
                 pltpu.VMEM((n * SEND, width), jnp.bfloat16),
                 pltpu.VMEM((n, SEND, width), jnp.bfloat16),
-                pltpu.VMEM(tile, jnp.float32),
-                pltpu.VMEM((n,) + tile, jnp.float32),
+                pltpu.VMEM((n // PER, CL_DEV, PER * CAP), jnp.float32),
+                pltpu.VMEM((n, CL_DEV, PER * CAP), jnp.float32),
                 pltpu.SemaphoreType.DMA((n,)),
                 pltpu.SemaphoreType.DMA((n,)),
                 pltpu.SemaphoreType.DMA((n,)),

time: 68 us -> 67.4 us (level)
  no operation moved by 1% of the time
where the time goes in v3:
time: 67.4 us; the launch traced here: 67.2 us
  Pallas kernels  66 us (98%)
  other arithmetic  1.26 us (2%)
    pallas_call x1, Pallas kernels, local(): pl.pallas_call(functools.partial(kernel, n, rows), out_shape=jax.ShapeDty...  66 us

profile of v3, /device:TPU:0, one launch (start us, length us, event | category | flops | bytes accessed | tf_op | source)
XLA Modules:
  0.0 67.2 jit_solution(4174242200223185459)
XLA Ops:
  0.0 66.0 %shard_map.28 = f32[1,512]{1,0:T(1,128)} custom-call(bf16[512,1152]{1,0:T(8,128)(2,1)} %emb_ref.1, s32[1,512]{1,0:T(1,128)} %bitcast.2), custom_call_target="tpu_custom_call" | custom-call | tf_op jit(solution)/shard_map/pallas_call | solution.py:159
  66.0 1.3 %broadcast_maximum_fusion = f32[1,512]{1,0:T(1,128)} fusion(f32[1,512]{1,0:T(1,128)} %shard_map.28), kind=kLoop, calls=%fused_computation | loop fusion | flops 512 | bytes 4096 | tf_op jit(solution)/shard_map/max | solution.py:179
